TPU v7x, 32 devices: a whole 2x2x4 slice. The times are simulated.
32 devices in a mesh: tile: 8 (over y, x, core), freq: 4 (over z).
Axes of the slice: x: 2, y: 2, z: 4, core: 2. Of those that a mesh axis runs over, the one named last changes fastest.
Arguments:
- data_spectrum: float32 [2, 32, 512, 1024], P(None, 'freq', 'tile'), may hold values from -24 to 24
- velocity_level: int32 [512, 1024], P('tile'), may hold values from 0 to 11
Outputs:
- primaries: float32 [64, 512, 1024], P(None, 'tile', 'freq')
- multiples: float32 [64, 512, 1024], P(None, 'tile', 'freq')
All inputs are finite; a program needn't handle non-finite values.
Results may differ from a plain program's by a relative error of at most 0.0003.
Values sent between devices are 32-bit elements; how exact they have to be, the bound alone decides.
A program may use at most 128 MiB of HBM per device.

v0:
```python
import functools
import math

import jax
import jax.numpy as jnp
import ml_dtypes
import numpy as np
from jax import lax
from jax.experimental import pallas as pl
from jax.experimental.pallas import tpu as pltpu
from jax.sharding import PartitionSpec as P

GROUPS = 3
PASSES = 3
STEPS = 4 * GROUPS

damping = 0.2
paraxial_top = 0.1
depth_step = 10.0
cell_width = 12.5
step_size = 0.6
energy_floor = 1e-05
filter_reach = 2

HALO = 16
LANES = 128
STRIDE = 100
OUTSIDE = 127
MESH = pl.DeviceIdType.MESH


def tile_count(width):
    count = 1
    while STRIDE * count < width + filter_reach + 1:
        count += 1
    return count


def overlapped(pieces, tile, lane):
    origin = STRIDE * tile - HALO + LANES
    k, off = origin // LANES, origin % LANES
    turn = LANES - off
    axis = pieces[0].ndim - 1
    return jnp.where(
        lane < turn, pltpu.roll(pieces[k], turn, axis), pltpu.roll(pieces[k + 1], turn, axis)
    )


def coefficient_table(orders, nz, per_chunk, chunks):
    table = np.zeros((chunks, 4, 8, LANES), np.float64)
    velocity = 1500.0 + 250.0 * np.arange(OUTSIDE)
    for j in range(chunks):
        for s in range(nz):
            for i in range(per_chunk):
                k = s * (orders // nz) + j * per_chunk + i
                omega = 4.0 * math.pi * (k + 1)
                theta = omega * depth_step / velocity
                q = velocity / (omega * cell_width)
                spread = damping + 1j * paraxial_top * q / (1.0 + q)
                turn = np.exp(1j * theta)
                centre = turn * (1.0 - 4.0 * spread)
                beside = turn * spread
                table[j, :, s * per_chunk + i, :OUTSIDE] = np.stack(
                    [centre.real, centre.imag, beside.real, beside.imag]
                )
    return table.astype(np.float32)


def trace_basis(orders, nz, per_chunk, chunks):
    samples = 2 * orders
    times = np.arange(samples)[:, None] + 0.5
    order = [
        s * (orders // nz) + j * per_chunk + i
        for j in range(chunks)
        for s in range(nz)
        for i in range(per_chunk)
    ]
    angles = 2.0 * math.pi * (np.array(order)[None, :] + 1.0) * times / samples
    basis = np.concatenate([np.cos(angles), -np.sin(angles)], axis=1) / math.sqrt(orders)
    basis = basis.astype(np.float32)
    high = basis.astype(ml_dtypes.bfloat16)
    low = (basis - high.astype(np.float32)).astype(ml_dtypes.bfloat16)
    return np.concatenate([high, high, low, low], axis=1)


def predict_kernel(
    tiles, nz, per_chunk, chunks, rows, width,
    x_ref, strip_ref, level_ref, table_ref,
    m_ref, d_ref,
    ext, sext, lext, index, coef, state,
    a_send, a_recv, s_send, s_recv, r_send, r_recv, q_send, q_recv, l_send, l_recv, own,
):
    tile = lax.axis_index("tile")
    me = lax.axis_index("freq")
    has_up = tile > 0
    has_down = tile < tiles - 1
    nt = tile_count(width)
    mains = width // LANES
    full = rows + 2 * HALO
    inner = pl.ds(HALO, rows)
    window = pl.ds(pl.multiple_of(me * width, LANES), width + 2 * LANES)

    barrier = pltpu.get_barrier_semaphore()
    for hop in range(1, nz):
        pl.semaphore_signal(
            barrier, inc=1, device_id=(tile, lax.rem(me + hop, nz)), device_id_type=MESH
        )

    @pl.when(has_up)
    def _():
        pl.semaphore_signal(barrier, inc=1, device_id=(tile - 1, me), device_id_type=MESH)

    @pl.when(has_down)
    def _():
        pl.semaphore_signal(barrier, inc=1, device_id=(tile + 1, me), device_id_type=MESH)

    pl.semaphore_wait(
        barrier, nz - 1 + has_up.astype(jnp.int32) + has_down.astype(jnp.int32)
    )

    def level_copy(up):
        src = level_ref.at[pl.ds(0 if up else rows - HALO, HALO), window]
        dst = lext.at[pl.ds(HALO + rows if up else 0, HALO), :]
        way = 0 if up else 1
        return pltpu.make_async_remote_copy(
            src_ref=src, dst_ref=dst, send_sem=l_send.at[way], recv_sem=l_recv.at[way],
            device_id=(tile + (-1 if up else 1), me), device_id_type=MESH,
        )

    def main_copy(j, dest, source):
        return pltpu.make_async_remote_copy(
            src_ref=x_ref.at[
                :, pl.ds(j * per_chunk, per_chunk), :,
                pl.ds(pl.multiple_of(dest * width, LANES), width),
            ],
            dst_ref=ext.at[j, :, pl.ds(source * per_chunk, per_chunk), inner, :],
            send_sem=a_send.at[j, dest], recv_sem=a_recv.at[j, source],
            device_id=(tile, dest), device_id_type=MESH,
        )

    def strip_copy(j, dest, source):
        return pltpu.make_async_remote_copy(
            src_ref=strip_ref.at[dest, j],
            dst_ref=sext.at[j, source, inner, :],
            send_sem=s_send.at[j, dest], recv_sem=s_recv.at[j, source],
            device_id=(tile, dest), device_id_type=MESH,
        )

    def row_copies(j, up):
        src = pl.ds(HALO if up else rows, HALO)
        dst = pl.ds(HALO + rows if up else 0, HALO)
        way = 0 if up else 1
        target = (tile + (-1 if up else 1), me)
        return (
            pltpu.make_async_remote_copy(
                src_ref=ext.at[j, :, :, src, :], dst_ref=ext.at[j, :, :, dst, :],
                send_sem=r_send.at[j, way], recv_sem=r_recv.at[j, way],
                device_id=target, device_id_type=MESH,
            ),
            pltpu.make_async_remote_copy(
                src_ref=sext.at[j, :, src, :], dst_ref=sext.at[j, :, dst, :],
                send_sem=q_send.at[j, way], recv_sem=q_recv.at[j, way],
                device_id=target, device_id_type=MESH,
            ),
        )

    def own_copies(j):
        return (
            pltpu.make_async_copy(
                x_ref.at[
                    :, pl.ds(j * per_chunk, per_chunk), :,
                    pl.ds(pl.multiple_of(me * width, LANES), width),
                ],
                ext.at[j, :, pl.ds(me * per_chunk, per_chunk), inner, :],
                own.at[j, 0],
            ),
            pltpu.make_async_copy(
                strip_ref.at[me, j], sext.at[j, me, inner, :], own.at[j, 1]
            ),
        )

    own_level = pltpu.make_async_copy(
        level_ref.at[:, window], lext.at[inner, :], own.at[chunks, 0]
    )

    @pl.when(has_up)
    def _():
        level_copy(True).start()

    @pl.when(has_down)
    def _():
        level_copy(False).start()

    own_level.start()

    def send(j, carry):
        for hop in range(1, nz):
            dest = lax.rem(me + hop, nz)
            strip_copy(j, dest, me).start()
            main_copy(j, dest, me).start()
        for copy in own_copies(j):
            copy.start()
        return carry

    lax.fori_loop(0, chunks, send, 0)

    top, bottom = pl.ds(0, HALO), pl.ds(HALO + rows, HALO)
    for missing, edge in ((jnp.logical_not(has_up), top), (jnp.logical_not(has_down), bottom)):

        @pl.when(missing)
        def _(edge=edge):
            lext[edge, :] = jnp.full((HALO, lext.shape[1]), OUTSIDE, jnp.int32)

            def clear(j, carry):
                for part in range(2):
                    for f in range(8):
                        ext[j, part, f, edge, :] = jnp.zeros((HALO, width), jnp.float32)
                for s in range(nz):
                    sext[j, s, edge, :] = jnp.zeros((HALO, LANES), jnp.float32)
                return carry

            lax.fori_loop(0, chunks, clear, 0)

    own_level.wait()

    @pl.when(has_up)
    def _():
        level_copy(True).wait_send()
        level_copy(False).wait_recv()

    @pl.when(has_down)
    def _():
        level_copy(False).wait_send()
        level_copy(True).wait_recv()

    lane2 = lax.broadcasted_iota(jnp.int32, (8, LANES), 1)
    lane3 = lax.broadcasted_iota(jnp.int32, (8, 8, LANES), 2)

    def make_index(b, carry):
        at = pl.ds(pl.multiple_of(b * 8, 8), 8)
        pieces = [lext[at, k * LANES : (k + 1) * LANES] for k in range(mains + 2)]
        for t in range(nt):
            found = overlapped(pieces, t, lane2)
            index[t, at] = jnp.broadcast_to(found[:, None, :], (8, 8, LANES))
        return carry

    lax.fori_loop(0, full // 8, make_index, 0)

    def one_chunk(j, carry):
        for copy in own_copies(j):
            copy.wait()
        for hop in range(1, nz):
            source = lax.rem(me + hop, nz)
            main_copy(j, me, source).wait_recv()
            strip_copy(j, me, source).wait_recv()

        @pl.when(has_up)
        def _():
            for copy in row_copies(j, True):
                copy.start()

        @pl.when(has_down)
        def _():
            for copy in row_copies(j, False):
                copy.start()

        def make_coef(e, carry):
            for t in range(nt):
                at = index[t, e]
                for c in range(4):
                    coef[c, t, e] = jnp.take_along_axis(
                        table_ref[j, c], at, axis=1, mode="promise_in_bounds"
                    )
            return carry

        lax.fori_loop(0, full, make_coef, 0)

        @pl.when(has_up)
        def _():
            for copy in row_copies(j, False):
                copy.wait_recv()

        @pl.when(has_down)
        def _():
            for copy in row_copies(j, True):
                copy.wait_recv()

        def fill(b, carry):
            at = pl.ds(pl.multiple_of(b * 8, 8), 8)
            for part in range(2):
                main = [
                    jnp.swapaxes(ext[j, part, :, at, k * LANES : (k + 1) * LANES], 0, 1)
                    for k in range(mains)
                ]
                strips = []
                for s in range(nz):
                    strip = sext[j, s, at, :]
                    for i in range(per_chunk):
                        base = (part * per_chunk + i) * 2 * HALO
                        strips.append(pltpu.roll(strip, (LANES - base - HALO) % LANES, 1))
                strip = jnp.swapaxes(jnp.stack(strips), 0, 1)
                pieces = [strip] + main + [strip]
                for t in range(nt):
                    state[0, part, t, at] = overlapped(pieces, t, lane3)

                @pl.when((b >= HALO // 8) & (b < (HALO + rows) // 8))
                def _():
                    for k in range(mains):
                        for r in range(8):
                            d_ref[b * 8 - HALO + r, k, part, j] = main[k][r]
            return carry

        lax.fori_loop(0, full // 8, fill, 0)

        def one_step(s, carry):
            old = lax.rem(s + 1, 2)
            new = lax.rem(s, 2)
            first = HALO - filter_reach - STEPS + s
            count = rows + 2 * (filter_reach + STEPS) - 2 * s

            def block(b, carry):
                e = first + 4 * b
                for t in range(nt):
                    re = [state[old, 0, t, e - 1 + r] for r in range(6)]
                    im = [state[old, 1, t, e - 1 + r] for r in range(6)]
                    for r in range(4):
                        a, b_ = re[r + 1], im[r + 1]
                        nr = (re[r] + re[r + 2]) + (
                            pltpu.roll(a, 1, 1) + pltpu.roll(a, LANES - 1, 1)
                        )
                        ni = (im[r] + im[r + 2]) + (
                            pltpu.roll(b_, 1, 1) + pltpu.roll(b_, LANES - 1, 1)
                        )
                        cr, ci = coef[0, t, e + r], coef[1, t, e + r]
                        br, bi = coef[2, t, e + r], coef[3, t, e + r]
                        state[new, 0, t, e + r] = (cr * a - ci * b_) + (br * nr - bi * ni)
                        state[new, 1, t, e + r] = (cr * b_ + ci * a) + (br * ni + bi * nr)
                return carry

            lax.fori_loop(0, (count + 3) // 4, block, 0)
            return carry

        lax.fori_loop(1, STEPS + 1, one_step, 0)

        def put(r, carry):
            for t in range(nt):
                for part in range(2):
                    m_ref[r, t, part, j] = state[STEPS % 2, part, t, r + HALO - filter_reach]
            return carry

        lax.fori_loop(0, rows + 2 * filter_reach, put, 0)
        return carry

    lax.fori_loop(0, chunks, one_chunk, 0)

    def finish(j, carry):
        for hop in range(1, nz):
            dest = lax.rem(me + hop, nz)
            strip_copy(j, dest, me).wait_send()
            main_copy(j, dest, me).wait_send()

        @pl.when(has_up)
        def _():
            for copy in row_copies(j, True):
                copy.wait_send()

        @pl.when(has_down)
        def _():
            for copy in row_copies(j, False):
                copy.wait_send()

        return carry

    lax.fori_loop(0, chunks, finish, 0)


def to_trace(basis, spectrum):
    high = spectrum.astype(jnp.bfloat16)
    low = (spectrum - high.astype(jnp.float32)).astype(jnp.bfloat16)
    both = jnp.concatenate([high, low, high, low], axis=0)
    return jnp.dot(basis, both, preferred_element_type=jnp.float32)


def subtract_kernel(rows, width, m_ref, d_ref, basis_ref, p_ref, q_ref, shifted, data, result):
    i = pl.program_id(0)
    mains = width // LANES
    nt = m_ref.shape[1]
    reach = filter_reach
    diameter = 2 * reach + 1
    samples = basis_ref.shape[0]
    basis = basis_ref[...]
    lane = lax.broadcasted_iota(jnp.int32, (samples, LANES), 1)

    def make_row(r, carry):
        spectrum = jnp.concatenate(
            [m_ref[r, t].reshape(samples, LANES) for t in range(nt)], axis=1
        )
        traces = -to_trace(basis, spectrum)
        for shift in range(diameter):
            for b in range(mains):
                low = LANES * b + shift - reach
                value = None
                for t in range(nt):
                    begin, end = STRIDE * t - reach, STRIDE * (t + 1) - reach
                    if end <= low or begin >= low + LANES:
                        continue
                    tile = traces[:, t * LANES : (t + 1) * LANES]
                    turn = (STRIDE * t - HALO - low) % LANES
                    moved = pltpu.roll(tile, turn, 1) if turn else tile
                    value = moved if value is None else jnp.where(lane < begin - low, value, moved)
                shifted[shift, r, :, b * LANES : (b + 1) * LANES] = value
        return carry

    lax.fori_loop(jnp.where(i == 0, 0, 8 * i + 2 * reach), 8 * i + 8 + 2 * reach, make_row, 0)

    def make_data(r, carry):
        spectrum = jnp.concatenate(
            [d_ref[8 * i + r, b].reshape(samples, LANES) for b in range(mains)], axis=1
        )
        data[r] = to_trace(basis, spectrum)
        return carry

    lax.fori_loop(0, 8, make_data, 0)

    taps = [(a, c) for a in range(diameter) for c in range(diameter)]

    def one_row(n, carry):
        r, b = n // mains, lax.rem(n, mains)
        at = pl.ds(pl.multiple_of(b * LANES, LANES), LANES)

        def tap(a, c):
            return shifted[c, 8 * i + r + a, :, at]

        recorded = data[r, :, at]

        def total(values):
            return jnp.sum(values, axis=0, keepdims=True)

        power = jnp.zeros((8, LANES), jnp.float32)
        for a, c in taps:
            value = tap(a, c)
            power = power + jnp.sum((value * value).reshape(samples // 8, 8, LANES), axis=0)
        gain = step_size / (energy_floor + total(power))
        weights = None
        for repeat in range(PASSES):
            residual = recorded
            if weights is not None:
                for weight, (a, c) in zip(weights, taps):
                    residual = residual - weight * tap(a, c)
            change = [total(residual * tap(a, c)) * gain for a, c in taps]
            weights = (
                change if weights is None else [w + more for w, more in zip(weights, change)]
            )
        residual = recorded
        for weight, (a, c) in zip(weights, taps):
            residual = residual - weight * tap(a, c)
        result[r, :, at] = residual
        return carry

    lax.fori_loop(0, 8 * mains, one_row, 0)

    for k in range(samples // 8):
        part = slice(8 * k, 8 * k + 8)
        p_ref[part] = jnp.swapaxes(result[:, part, :], 0, 1)
        q_ref[part] = jnp.swapaxes(
            shifted[reach, pl.ds(8 * i + reach, 8), part, :], 0, 1
        )


def local(mesh_shape, data_spectrum, velocity_level):
    nz, tiles = mesh_shape["freq"], mesh_shape["tile"]
    _, local_freqs, rows, cols = data_spectrum.shape
    orders = local_freqs * nz
    samples = 2 * orders
    width = cols // nz
    per_chunk = 8 // nz
    chunks = local_freqs // per_chunk
    nt = tile_count(width)
    mains = width // LANES
    full = rows + 2 * HALO
    reach = filter_reach

    around = jnp.pad(data_spectrum, ((0, 0), (0, 0), (0, 0), (HALO, HALO)))
    strips = jnp.stack(
        [
            jnp.concatenate(
                [
                    around[..., d * width : d * width + HALO],
                    around[..., (d + 1) * width + HALO : (d + 1) * width + 2 * HALO],
                ],
                axis=-1,
            )
            for d in range(nz)
        ]
    )
    strips = strips.reshape(nz, 2, chunks, per_chunk, rows, 2 * HALO)
    strips = strips.transpose(0, 2, 4, 1, 3, 5).reshape(nz, chunks, rows, -1)
    strips = jnp.pad(strips, ((0, 0),) * 3 + ((0, LANES - strips.shape[-1]),))
    levels = jnp.pad(velocity_level, ((0, 0), (LANES, LANES)), constant_values=OUTSIDE)
    table = jnp.asarray(coefficient_table(orders, nz, per_chunk, chunks))
    basis = jnp.asarray(trace_basis(orders, nz, per_chunk, chunks))

    dma = pltpu.SemaphoreType.DMA
    vmem = pl.BlockSpec(memory_space=pltpu.VMEM)
    hbm = pl.BlockSpec(memory_space=pl.ANY)
    predicted, recorded = pl.pallas_call(
        functools.partial(predict_kernel, tiles, nz, per_chunk, chunks, rows, width),
        out_shape=(
            jax.ShapeDtypeStruct((rows + 2 * reach, nt, 2, chunks, 8, LANES), jnp.float32),
            jax.ShapeDtypeStruct((rows, mains, 2, chunks, 8, LANES), jnp.float32),
        ),
        in_specs=[hbm, hbm, hbm, vmem],
        out_specs=(vmem, vmem),
        scratch_shapes=[
            pltpu.VMEM((chunks, 2, 8, full, width), jnp.float32),
            pltpu.VMEM((chunks, nz, full, LANES), jnp.float32),
            pltpu.VMEM((full, width + 2 * LANES), jnp.int32),
            pltpu.VMEM((nt, full, 8, LANES), jnp.int32),
            pltpu.VMEM((4, nt, full, 8, LANES), jnp.float32),
            pltpu.VMEM((2, 2, nt, full, 8, LANES), jnp.float32),
            dma((chunks, nz)), dma((chunks, nz)), dma((chunks, nz)), dma((chunks, nz)),
            dma((chunks, 2)), dma((chunks, 2)), dma((chunks, 2)), dma((chunks, 2)),
            dma((2,)), dma((2,)), dma((chunks + 1, 2)),
        ],
        compiler_params=pltpu.CompilerParams(
            collective_id=0, has_side_effects=True, vmem_limit_bytes=56 * 2**20
        ),
        name="predict",
    )(data_spectrum, strips, levels, table)

    block = pl.BlockSpec((samples, 8, width), lambda i: (0, i, 0))
    out = jax.ShapeDtypeStruct((samples, rows, width), jnp.float32)
    return pl.pallas_call(
        functools.partial(subtract_kernel, rows, width),
        grid=(rows // 8,),
        out_shape=(out, out),
        in_specs=[vmem, vmem, vmem],
        out_specs=(block, block),
        scratch_shapes=[
            pltpu.VMEM((2 * reach + 1, rows + 2 * reach, samples, width), jnp.float32),
            pltpu.VMEM((8, samples, width), jnp.float32),
            pltpu.VMEM((8, samples, width), jnp.float32),
        ],
        compiler_params=pltpu.CompilerParams(vmem_limit_bytes=56 * 2**20),
        name="subtract",
    )(predicted, recorded, basis)


def solution(mesh):
    in_specs = (P(None, "freq", "tile", None), P("tile", None))
    out_specs = (P(None, "tile", "freq"), P(None, "tile", "freq"))
    return jax.shard_map(
        functools.partial(local, dict(mesh.shape)),
        mesh=mesh, in_specs=in_specs, out_specs=out_specs, check_vma=False,
    )
```

profile of v0, /device:TPU:11, one launch (start us, length us, event | category | flops | bytes accessed | tf_op | source)
XLA Modules:
  0.0 467.7 jit_solution(17181584907360113979)
XLA Ops:
  0.6 1.7 pad.8.level_ref
  2.3 2.4 fusion
  4.7 0.2 concatenate.13
  5.0 0.2 copy.13
  5.2 0.9 copy.10
  6.1 0.3 pad_maximum_fusion.1
  6.4 0.2 copy.11
  6.6 0.2 copy.12
  6.8 1.1 pad_maximum_fusion
  7.9 1.1 copy.14.strip_ref
  9.0 359.3 %predict.1 = (f32[68,3,2,4,8,128]{5,4,3,2,1,0:T(8,128)}, f32[64,2,2,4,8,128]{5,4,3,2,1,0:T(8,128)}) custom-call(f32[2,8,64,1024]{3,2,1,0:T(8,128)} %x_ref.1, f32[4,4,64,128]{3,2,1,0:T(8,128)} %copy.14.strip_ref, s32[64,1280]{1,0:T(8,128)} %pad.8.level_ref, f32[4,4,8,128]{3,2,1,0:T(8,128)} %constant.9.clone.table_ref), custom_call_target="tpu_custom_call" | custom-call | tf_op jit(solution)/shard_map/predict/pallas_call | solution.py:506
  368.4 99.3 %subtract.1 = (f32[64,64,256]{2,1,0:T(8,128)}, f32[64,64,256]{2,1,0:T(8,128)}) custom-call(f32[68,3,2,4,8,128]{5,4,3,2,1,0:T(8,128)} %get-tuple-element.4.m_ref, f32[64,2,2,4,8,128]{5,4,3,2,1,0:T(8,128)} %get-tuple-element.5.d_ref, bf16[64,256]{1,0:T(8,128)(2,1)} %constant.10.clone.basis_ref), custom_call_target="tpu_custom_call" | custom-call | tf_op jit(solution)/shard_map/subtract/pallas_call | solution.py:533
  (1 shorter events, 0.0 us)
where the time goes:
time: 469 us; the launch traced here: 468 us
  Pallas kernels  459 us (98%)
  local copies, waits for them, and re-layouts  6.93 us (1%)
    pallas_call x1, Pallas kernels, local(): pl.pallas_call(functools.partial(predict_kernel, tiles, nz, per_chunk, ch...  359 us
    pallas_call x1, Pallas kernels, local(): pl.pallas_call(functools.partial(subtract_kernel, rows, width), grid=(row...  99.3 us

commit v1 on v0

--- a/solution.py
+++ b/solution.py
@@ -24,6 +24,7 @@
 
 HALO = 16
 LANES = 128
+ROWS = 8
 STRIDE = 100
 OUTSIDE = 127
 MESH = pl.DeviceIdType.MESH
@@ -87,7 +88,7 @@
     tiles, nz, per_chunk, chunks, rows, width,
     x_ref, strip_ref, level_ref, table_ref,
     m_ref, d_ref,
-    ext, sext, lext, index, coef, state,
+    ext, sext, lext, index, coef, state, other,
     a_send, a_recv, s_send, s_recv, r_send, r_recv, q_send, q_recv, l_send, l_recv, own,
 ):
     tile = lax.axis_index("tile")
@@ -264,16 +265,18 @@
             for copy in row_copies(j, False):
                 copy.start()
 
-        def make_coef(e, carry):
-            for t in range(nt):
-                at = index[t, e]
-                for c in range(4):
-                    coef[c, t, e] = jnp.take_along_axis(
-                        table_ref[j, c], at, axis=1, mode="promise_in_bounds"
-                    )
+        def make_coef(b, carry):
+            values = [table_ref[j, c] for c in range(4)]
+            for r in range(8):
+                for t in range(nt):
+                    at = index[t, 8 * b + r]
+                    for c in range(4):
+                        coef[c, t, 8 * b + r] = jnp.take_along_axis(
+                            values[c], at, axis=1, mode="promise_in_bounds"
+                        )
             return carry
 
-        lax.fori_loop(0, full, make_coef, 0)
+        lax.fori_loop(0, full // 8, make_coef, 0)
 
         @pl.when(has_up)
         def _():
@@ -301,7 +304,7 @@
                 strip = jnp.swapaxes(jnp.stack(strips), 0, 1)
                 pieces = [strip] + main + [strip]
                 for t in range(nt):
-                    state[0, part, t, at] = overlapped(pieces, t, lane3)
+                    state[part, t, at] = overlapped(pieces, t, lane3)
 
                 @pl.when((b >= HALO // 8) & (b < (HALO + rows) // 8))
                 def _():
@@ -312,18 +315,16 @@
 
         lax.fori_loop(0, full // 8, fill, 0)
 
-        def one_step(s, carry):
-            old = lax.rem(s + 1, 2)
-            new = lax.rem(s, 2)
+        def one_step(s, old, new):
             first = HALO - filter_reach - STEPS + s
             count = rows + 2 * (filter_reach + STEPS) - 2 * s
 
             def block(b, carry):
-                e = first + 4 * b
+                e = first + ROWS * b
                 for t in range(nt):
-                    re = [state[old, 0, t, e - 1 + r] for r in range(6)]
-                    im = [state[old, 1, t, e - 1 + r] for r in range(6)]
-                    for r in range(4):
+                    re = [old[0, t, e - 1 + r] for r in range(ROWS + 2)]
+                    im = [old[1, t, e - 1 + r] for r in range(ROWS + 2)]
+                    for r in range(ROWS):
                         a, b_ = re[r + 1], im[r + 1]
                         nr = (re[r] + re[r + 2]) + (
                             pltpu.roll(a, 1, 1) + pltpu.roll(a, LANES - 1, 1)
@@ -333,22 +334,29 @@
                         )
                         cr, ci = coef[0, t, e + r], coef[1, t, e + r]
                         br, bi = coef[2, t, e + r], coef[3, t, e + r]
-                        state[new, 0, t, e + r] = (cr * a - ci * b_) + (br * nr - bi * ni)
-                        state[new, 1, t, e + r] = (cr * b_ + ci * a) + (br * ni + bi * nr)
+                        new[0, t, e + r] = (cr * a - ci * b_) + (br * nr - bi * ni)
+                        new[1, t, e + r] = (cr * b_ + ci * a) + (br * ni + bi * nr)
                 return carry
 
-            lax.fori_loop(0, (count + 3) // 4, block, 0)
+            lax.fori_loop(0, (count + ROWS - 1) // ROWS, block, 0)
+
+        def two_steps(n, carry):
+            one_step(2 * n + 1, state, other)
+            one_step(2 * n + 2, other, state)
             return carry
 
-        lax.fori_loop(1, STEPS + 1, one_step, 0)
-
-        def put(r, carry):
-            for t in range(nt):
-                for part in range(2):
-                    m_ref[r, t, part, j] = state[STEPS % 2, part, t, r + HALO - filter_reach]
+        lax.fori_loop(0, STEPS // 2, two_steps, 0)
+
+        def put(b, carry):
+            for r in range(4):
+                for t in range(nt):
+                    for part in range(2):
+                        m_ref[4 * b + r, t, part, j] = state[
+                            part, t, 4 * b + r + HALO - filter_reach
+                        ]
             return carry
 
-        lax.fori_loop(0, rows + 2 * filter_reach, put, 0)
+        lax.fori_loop(0, rows // 4 + filter_reach // 2, put, 0)
         return carry
 
     lax.fori_loop(0, chunks, one_chunk, 0)
@@ -516,8 +524,9 @@
             pltpu.VMEM((chunks, nz, full, LANES), jnp.float32),
             pltpu.VMEM((full, width + 2 * LANES), jnp.int32),
             pltpu.VMEM((nt, full, 8, LANES), jnp.int32),
-            pltpu.VMEM((4, nt, full, 8, LANES), jnp.float32),
-            pltpu.VMEM((2, 2, nt, full, 8, LANES), jnp.float32),
+            pltpu.VMEM((4, nt, full + ROWS, 8, LANES), jnp.float32),
+            pltpu.VMEM((2, nt, full + ROWS, 8, LANES), jnp.float32),
+            pltpu.VMEM((2, nt, full + ROWS, 8, LANES), jnp.float32),
             dma((chunks, nz)), dma((chunks, nz)), dma((chunks, nz)), dma((chunks, nz)),
             dma((chunks, 2)), dma((chunks, 2)), dma((chunks, 2)), dma((chunks, 2)),
             dma((2,)), dma((2,)), dma((chunks + 1, 2)),

time: 469 us -> 295 us (0.63)
  Pallas kernels: 459 us -> 284 us
    pallas_call x1, Pallas kernels: 359 us -> 184 us  [local(): pl.pallas_call(functools.partial(predict_kernel, tiles, nz, per_chunk, ch...]
where the time goes in v1:
time: 295 us; the launch traced here: 293 us
  Pallas kernels  284 us (96%)
  local copies, waits for them, and re-layouts  6.93 us (2%)
    pallas_call x1, Pallas kernels, local(): pl.pallas_call(functools.partial(predict_kernel, tiles, nz, per_chunk, ch...  184 us
    pallas_call x1, Pallas kernels, local(): pl.pallas_call(functools.partial(subtract_kernel, rows, width), grid=(row...  99.3 us

profile of v1, /device:TPU:11, one launch (start us, length us, event | category | flops | bytes accessed | tf_op | source)
XLA Modules:
  0.0 292.6 jit_solution(215267593921278820)
XLA Ops:
  0.6 1.7 pad.8.level_ref
  2.3 2.4 fusion
  4.7 0.2 concatenate.13
  5.0 0.2 copy.13
  5.2 0.9 copy.10
  6.1 0.3 pad_maximum_fusion.1
  6.4 0.2 copy.11
  6.6 0.2 copy.12
  6.8 1.1 pad_maximum_fusion
  7.9 1.1 copy.14.strip_ref
  9.0 184.3 %predict.1 = (f32[68,3,2,4,8,128]{5,4,3,2,1,0:T(8,128)}, f32[64,2,2,4,8,128]{5,4,3,2,1,0:T(8,128)}) custom-call(f32[2,8,64,1024]{3,2,1,0:T(8,128)} %x_ref.1, f32[4,4,64,128]{3,2,1,0:T(8,128)} %copy.14.strip_ref, s32[64,1280]{1,0:T(8,128)} %pad.8.level_ref, f32[4,4,8,128]{3,2,1,0:T(8,128)} %constant.9.clone.table_ref), custom_call_target="tpu_custom_call" | custom-call | tf_op jit(solution)/shard_map/predict/pallas_call | solution.py:514
  193.3 99.3 %subtract.1 = (f32[64,64,256]{2,1,0:T(8,128)}, f32[64,64,256]{2,1,0:T(8,128)}) custom-call(f32[68,3,2,4,8,128]{5,4,3,2,1,0:T(8,128)} %get-tuple-element.4.m_ref, f32[64,2,2,4,8,128]{5,4,3,2,1,0:T(8,128)} %get-tuple-element.5.d_ref, bf16[64,256]{1,0:T(8,128)(2,1)} %constant.10.clone.basis_ref), custom_call_target="tpu_custom_call" | custom-call | tf_op jit(solution)/shard_map/subtract/pallas_call | solution.py:542
  (1 shorter events, 0.0 us)

commit v2 on v1

--- a/solution.py
+++ b/solution.py
@@ -194,16 +194,26 @@
 
     own_level.start()
 
-    def send(j, carry):
+    def send(j):
         for hop in range(1, nz):
             dest = lax.rem(me + hop, nz)
             strip_copy(j, dest, me).start()
             main_copy(j, dest, me).start()
+
+    def sent(j):
+        for hop in range(1, nz):
+            dest = lax.rem(me + hop, nz)
+            strip_copy(j, dest, me).wait_send()
+            main_copy(j, dest, me).wait_send()
+
+    send(0)
+
+    def keep(j, carry):
         for copy in own_copies(j):
             copy.start()
         return carry
 
-    lax.fori_loop(0, chunks, send, 0)
+    lax.fori_loop(0, chunks, keep, 0)
 
     top, bottom = pl.ds(0, HALO), pl.ds(HALO + rows, HALO)
     for missing, edge in ((jnp.logical_not(has_up), top), (jnp.logical_not(has_down), bottom)):
@@ -248,6 +258,12 @@
     lax.fori_loop(0, full // 8, make_index, 0)
 
     def one_chunk(j, carry):
+        sent(j)
+
+        @pl.when(j + 1 < chunks)
+        def _():
+            send(j + 1)
+
         for copy in own_copies(j):
             copy.wait()
         for hop in range(1, nz):
@@ -356,17 +372,12 @@
                         ]
             return carry
 
-        lax.fori_loop(0, rows // 4 + filter_reach // 2, put, 0)
+        lax.fori_loop(0, (rows + 8) // 4, put, 0)
         return carry
 
     lax.fori_loop(0, chunks, one_chunk, 0)
 
     def finish(j, carry):
-        for hop in range(1, nz):
-            dest = lax.rem(me + hop, nz)
-            strip_copy(j, dest, me).wait_send()
-            main_copy(j, dest, me).wait_send()
-
         @pl.when(has_up)
         def _():
             for copy in row_copies(j, True):
@@ -389,7 +400,9 @@
     return jnp.dot(basis, both, preferred_element_type=jnp.float32)
 
 
-def subtract_kernel(rows, width, m_ref, d_ref, basis_ref, p_ref, q_ref, shifted, data, result):
+def subtract_kernel(
+    rows, width, m_ref, d_ref, basis_ref, p_ref, q_ref, shifted, power, data, residual, held
+):
     i = pl.program_id(0)
     mains = width // LANES
     nt = m_ref.shape[1]
@@ -397,82 +410,127 @@
     diameter = 2 * reach + 1
     samples = basis_ref.shape[0]
     basis = basis_ref[...]
-    lane = lax.broadcasted_iota(jnp.int32, (samples, LANES), 1)
-
-    def make_row(r, carry):
-        spectrum = jnp.concatenate(
-            [m_ref[r, t].reshape(samples, LANES) for t in range(nt)], axis=1
-        )
-        traces = -to_trace(basis, spectrum)
-        for shift in range(diameter):
-            for b in range(mains):
-                low = LANES * b + shift - reach
-                value = None
-                for t in range(nt):
-                    begin, end = STRIDE * t - reach, STRIDE * (t + 1) - reach
-                    if end <= low or begin >= low + LANES:
-                        continue
-                    tile = traces[:, t * LANES : (t + 1) * LANES]
-                    turn = (STRIDE * t - HALO - low) % LANES
-                    moved = pltpu.roll(tile, turn, 1) if turn else tile
-                    value = moved if value is None else jnp.where(lane < begin - low, value, moved)
-                shifted[shift, r, :, b * LANES : (b + 1) * LANES] = value
+    lane = lax.broadcasted_iota(jnp.int32, (8, 8, LANES), 2)
+
+    def traces(ref, first, count):
+        def two_rows(n, carry):
+            spectrum = jnp.concatenate(
+                [
+                    ref[first + 2 * n + r, t].reshape(samples, LANES)
+                    for r in range(2)
+                    for t in range(count)
+                ],
+                axis=1,
+            )
+            found = to_trace(basis, spectrum)
+            for r in range(2):
+                for t in range(count):
+                    k = r * count + t
+                    held[t, 2 * n + r] = found[:, k * LANES : (k + 1) * LANES]
+            return carry
+
+        lax.fori_loop(0, 4, two_rows, 0)
+
+    def make_block(k, carry):
+        traces(m_ref, 8 * k, nt)
+        here = pl.ds(pl.multiple_of(8 * k, 8), 8)
+
+        def some_times(n, sums):
+            at = pl.ds(pl.multiple_of(8 * n, 8), 8)
+            tiles = [-jnp.swapaxes(held[t, :, at, :], 0, 1) for t in range(nt)]
+            sums = list(sums)
+            for shift in range(diameter):
+                for b in range(mains):
+                    low = LANES * b + shift - reach
+                    value = None
+                    for t in range(nt):
+                        begin, end = STRIDE * t - reach, STRIDE * (t + 1) - reach
+                        if end <= low or begin >= low + LANES:
+                            continue
+                        turn = (STRIDE * t - HALO - low) % LANES
+                        moved = pltpu.roll(tiles[t], turn, 2) if turn else tiles[t]
+                        value = (
+                            moved
+                            if value is None
+                            else jnp.where(lane < begin - low, value, moved)
+                        )
+                    shifted[shift, at, b, here, :] = value
+                    sums[b] = sums[b] + jnp.sum(value * value, axis=0)
+            return tuple(sums)
+
+        zero = jnp.zeros((8, LANES), jnp.float32)
+        sums = lax.fori_loop(0, samples // 8, some_times, (zero,) * mains)
+        for b in range(mains):
+            power[b, here, :] = sums[b]
         return carry
 
-    lax.fori_loop(jnp.where(i == 0, 0, 8 * i + 2 * reach), 8 * i + 8 + 2 * reach, make_row, 0)
-
-    def make_data(r, carry):
-        spectrum = jnp.concatenate(
-            [d_ref[8 * i + r, b].reshape(samples, LANES) for b in range(mains)], axis=1
-        )
-        data[r] = to_trace(basis, spectrum)
+    lax.fori_loop(jnp.where(i == 0, 0, i + 1), i + 2, make_block, 0)
+
+    traces(d_ref, 8 * i, mains)
+
+    def turn_data(n, carry):
+        at = pl.ds(pl.multiple_of(8 * n, 8), 8)
+        for b in range(mains):
+            data[at, b] = jnp.swapaxes(held[b, :, at, :], 0, 1)
         return carry
 
-    lax.fori_loop(0, 8, make_data, 0)
+    lax.fori_loop(0, samples // 8, turn_data, 0)
 
     taps = [(a, c) for a in range(diameter) for c in range(diameter)]
 
-    def one_row(n, carry):
-        r, b = n // mains, lax.rem(n, mains)
+    def one_tile(b, carry):
+        def tap(t, a, c):
+            return shifted[c, t, b, pl.ds(8 * i + a, 8), :]
+
+        energy = energy_floor
+        for a in range(diameter):
+            energy = energy + power[b, pl.ds(8 * i + a, 8), :]
+        gain = step_size / energy
+
+        def match(read):
+            def some(n, sums):
+                sums = list(sums)
+                for u in range(2):
+                    t = 2 * n + u
+                    value = read(t)
+                    sums = [sums[k] + value * tap(t, a, c) for k, (a, c) in enumerate(taps)]
+                return tuple(sums)
+
+            zero = jnp.zeros((8, LANES), jnp.float32)
+            sums = lax.fori_loop(0, samples // 2, some, (zero,) * len(taps))
+            return [found * gain for found in sums]
+
+        def remove(weights, write):
+            def some(n, carry):
+                for u in range(2):
+                    t = 2 * n + u
+                    parts = [None] * diameter
+                    for weight, (a, c) in zip(weights, taps):
+                        term = weight * tap(t, a, c)
+                        parts[c] = term if parts[c] is None else parts[c] + term
+                    filtered = functools.reduce(jnp.add, parts)
+                    write(t, data[t, b] - filtered)
+                return carry
+
+            lax.fori_loop(0, samples // 2, some, 0)
+
+        def keep(t, value):
+            residual[t] = value
+
         at = pl.ds(pl.multiple_of(b * LANES, LANES), LANES)
 
-        def tap(a, c):
-            return shifted[c, 8 * i + r + a, :, at]
-
-        recorded = data[r, :, at]
-
-        def total(values):
-            return jnp.sum(values, axis=0, keepdims=True)
-
-        power = jnp.zeros((8, LANES), jnp.float32)
-        for a, c in taps:
-            value = tap(a, c)
-            power = power + jnp.sum((value * value).reshape(samples // 8, 8, LANES), axis=0)
-        gain = step_size / (energy_floor + total(power))
-        weights = None
-        for repeat in range(PASSES):
-            residual = recorded
-            if weights is not None:
-                for weight, (a, c) in zip(weights, taps):
-                    residual = residual - weight * tap(a, c)
-            change = [total(residual * tap(a, c)) * gain for a, c in taps]
-            weights = (
-                change if weights is None else [w + more for w, more in zip(weights, change)]
-            )
-        residual = recorded
-        for weight, (a, c) in zip(weights, taps):
-            residual = residual - weight * tap(a, c)
-        result[r, :, at] = residual
+        def put(t, value):
+            p_ref[t, :, at] = value
+            q_ref[t, :, at] = tap(t, reach, reach)
+
+        weights = match(lambda t: data[t, b])
+        for repeat in range(1, PASSES):
+            remove(weights, keep)
+            weights = [w + more for w, more in zip(weights, match(lambda t: residual[t]))]
+        remove(weights, put)
         return carry
 
-    lax.fori_loop(0, 8 * mains, one_row, 0)
-
-    for k in range(samples // 8):
-        part = slice(8 * k, 8 * k + 8)
-        p_ref[part] = jnp.swapaxes(result[:, part, :], 0, 1)
-        q_ref[part] = jnp.swapaxes(
-            shifted[reach, pl.ds(8 * i + reach, 8), part, :], 0, 1
-        )
+    lax.fori_loop(0, mains, one_tile, 0)
 
 
 def local(mesh_shape, data_spectrum, velocity_level):
@@ -514,7 +572,7 @@
     predicted, recorded = pl.pallas_call(
         functools.partial(predict_kernel, tiles, nz, per_chunk, chunks, rows, width),
         out_shape=(
-            jax.ShapeDtypeStruct((rows + 2 * reach, nt, 2, chunks, 8, LANES), jnp.float32),
+            jax.ShapeDtypeStruct((rows + 8, nt, 2, chunks, 8, LANES), jnp.float32),
             jax.ShapeDtypeStruct((rows, mains, 2, chunks, 8, LANES), jnp.float32),
         ),
         in_specs=[hbm, hbm, hbm, vmem],
@@ -546,9 +604,11 @@
         in_specs=[vmem, vmem, vmem],
         out_specs=(block, block),
         scratch_shapes=[
-            pltpu.VMEM((2 * reach + 1, rows + 2 * reach, samples, width), jnp.float32),
-            pltpu.VMEM((8, samples, width), jnp.float32),
-            pltpu.VMEM((8, samples, width), jnp.float32),
+            pltpu.VMEM((2 * reach + 1, samples, mains, rows + 8, LANES), jnp.float32),
+            pltpu.VMEM((mains, rows + 8, LANES), jnp.float32),
+            pltpu.VMEM((samples, mains, 8, LANES), jnp.float32),
+            pltpu.VMEM((samples, 8, LANES), jnp.float32),
+            pltpu.VMEM((nt, 8, samples, LANES), jnp.float32),
         ],
         compiler_params=pltpu.CompilerParams(vmem_limit_bytes=56 * 2**20),
         name="subtract",

time: 295 us -> 311 us (1.054)
  Pallas kernels: 284 us -> 302 us
    pallas_call x1, Pallas kernels: 99.3 us -> 121 us  [local(): pl.pallas_call(functools.partial(subtract_kernel, rows, width), grid=(row...]
    pallas_call x1, Pallas kernels: 184 us -> 181 us  [local(): pl.pallas_call(functools.partial(predict_kernel, tiles, nz, per_chunk, ch...]
where the time goes in v2:
time: 311 us
  Pallas kernels  302 us (97%)
  local copies, waits for them, and re-layouts  6.93 us (2%)
    pallas_call x1, Pallas kernels, local(): pl.pallas_call(functools.partial(predict_kernel, tiles, nz, per_chunk, ch...  181 us
    pallas_call x1, Pallas kernels, local(): pl.pallas_call(functools.partial(subtract_kernel, rows, width), grid=(row...  121 us

profile of v2, /device:TPU:11, one launch (start us, length us, event | category | flops | bytes accessed | tf_op | source)
XLA Modules:
  0.0 310.8 jit_solution(13332203416555104489)
XLA Ops:
  0.6 1.7 pad.8.level_ref
  2.3 2.4 fusion
  4.7 0.2 concatenate.13
  5.0 0.2 copy.13
  5.2 0.9 copy.10
  6.1 0.3 pad_maximum_fusion.1
  6.4 0.2 copy.11
  6.6 0.2 copy.12
  6.8 1.1 pad_maximum_fusion
  7.9 1.1 copy.14.strip_ref
  9.0 180.6 %predict.1 = (f32[72,3,2,4,8,128]{5,4,3,2,1,0:T(8,128)}, f32[64,2,2,4,8,128]{5,4,3,2,1,0:T(8,128)}) custom-call(f32[2,8,64,1024]{3,2,1,0:T(8,128)} %x_ref.1, f32[4,4,64,128]{3,2,1,0:T(8,128)} %copy.14.strip_ref, s32[64,1280]{1,0:T(8,128)} %pad.8.level_ref, f32[4,4,8,128]{3,2,1,0:T(8,128)} %constant.9.clone.table_ref), custom_call_target="tpu_custom_call" | custom-call | tf_op jit(solution)/shard_map/predict/pallas_call | solution.py:572
  189.7 121.2 %subtract.1 = (f32[64,64,256]{2,1,0:T(8,128)}, f32[64,64,256]{2,1,0:T(8,128)}) custom-call(f32[72,3,2,4,8,128]{5,4,3,2,1,0:T(8,128)} %get-tuple-element.4.m_ref, f32[64,2,2,4,8,128]{5,4,3,2,1,0:T(8,128)} %get-tuple-element.5.d_ref, bf16[64,256]{1,0:T(8,128)(2,1)} %constant.10.clone.basis_ref), custom_call_target="tpu_custom_call" | custom-call | tf_op jit(solution)/shard_map/subtract/pallas_call | solution.py:600
  (1 shorter events, 0.0 us)

commit v3 on v2

--- a/solution.py
+++ b/solution.py
@@ -24,7 +24,7 @@
 
 HALO = 16
 LANES = 128
-ROWS = 8
+ROWS = 12
 STRIDE = 100
 OUTSIDE = 127
 MESH = pl.DeviceIdType.MESH
@@ -257,7 +257,7 @@
 
     lax.fori_loop(0, full // 8, make_index, 0)
 
-    def one_chunk(j, carry):
+    def arrive(j):
         sent(j)
 
         @pl.when(j + 1 < chunks)
@@ -281,6 +281,9 @@
             for copy in row_copies(j, False):
                 copy.start()
 
+    arrive(0)
+
+    def one_chunk(j, carry):
         def make_coef(b, carry):
             values = [table_ref[j, c] for c in range(4)]
             for r in range(8):
@@ -337,26 +340,35 @@
 
             def block(b, carry):
                 e = first + ROWS * b
-                for t in range(nt):
-                    re = [old[0, t, e - 1 + r] for r in range(ROWS + 2)]
-                    im = [old[1, t, e - 1 + r] for r in range(ROWS + 2)]
-                    for r in range(ROWS):
-                        a, b_ = re[r + 1], im[r + 1]
-                        nr = (re[r] + re[r + 2]) + (
-                            pltpu.roll(a, 1, 1) + pltpu.roll(a, LANES - 1, 1)
+
+                def row(r):
+                    return [(old[0, t, e + r], old[1, t, e + r]) for t in range(nt)]
+
+                above, here = row(-1), row(0)
+                for r in range(ROWS):
+                    below = row(r + 1)
+                    for t in range(nt):
+                        p, q = here[t]
+                        nr = (above[t][0] + below[t][0]) + (
+                            pltpu.roll(p, 1, 1) + pltpu.roll(p, LANES - 1, 1)
                         )
-                        ni = (im[r] + im[r + 2]) + (
-                            pltpu.roll(b_, 1, 1) + pltpu.roll(b_, LANES - 1, 1)
+                        ni = (above[t][1] + below[t][1]) + (
+                            pltpu.roll(q, 1, 1) + pltpu.roll(q, LANES - 1, 1)
                         )
                         cr, ci = coef[0, t, e + r], coef[1, t, e + r]
                         br, bi = coef[2, t, e + r], coef[3, t, e + r]
-                        new[0, t, e + r] = (cr * a - ci * b_) + (br * nr - bi * ni)
-                        new[1, t, e + r] = (cr * b_ + ci * a) + (br * ni + bi * nr)
+                        new[0, t, e + r] = (cr * p - ci * q) + (br * nr - bi * ni)
+                        new[1, t, e + r] = (cr * q + ci * p) + (br * ni + bi * nr)
+                    above, here = here, below
                 return carry
 
             lax.fori_loop(0, (count + ROWS - 1) // ROWS, block, 0)
 
         def two_steps(n, carry):
+            @pl.when((n == STEPS // 2 - 1) & (j + 1 < chunks))
+            def _():
+                arrive(j + 1)
+
             one_step(2 * n + 1, state, other)
             one_step(2 * n + 2, other, state)
             return carry
@@ -403,134 +415,137 @@
 def subtract_kernel(
     rows, width, m_ref, d_ref, basis_ref, p_ref, q_ref, shifted, power, data, residual, held
 ):
-    i = pl.program_id(0)
-    mains = width // LANES
     nt = m_ref.shape[1]
     reach = filter_reach
     diameter = 2 * reach + 1
     samples = basis_ref.shape[0]
+    turns = rows // 8
     basis = basis_ref[...]
     lane = lax.broadcasted_iota(jnp.int32, (8, 8, LANES), 2)
 
-    def traces(ref, first, count):
-        def two_rows(n, carry):
+    def traces(ref, count, tiles):
+        def four_rows(n, carry):
             spectrum = jnp.concatenate(
-                [
-                    ref[first + 2 * n + r, t].reshape(samples, LANES)
-                    for r in range(2)
-                    for t in range(count)
-                ],
+                [ref[4 * n + r, t].reshape(samples, LANES) for r in range(4) for t in tiles],
                 axis=1,
             )
             found = to_trace(basis, spectrum)
-            for r in range(2):
-                for t in range(count):
-                    k = r * count + t
-                    held[t, 2 * n + r] = found[:, k * LANES : (k + 1) * LANES]
+            for r in range(4):
+                for k in range(len(tiles)):
+                    at = (r * len(tiles) + k) * LANES
+                    held[k, 4 * n + r] = found[:, at : at + LANES]
             return carry
 
-        lax.fori_loop(0, 4, two_rows, 0)
-
-    def make_block(k, carry):
-        traces(m_ref, 8 * k, nt)
-        here = pl.ds(pl.multiple_of(8 * k, 8), 8)
-
-        def some_times(n, sums):
-            at = pl.ds(pl.multiple_of(8 * n, 8), 8)
-            tiles = [-jnp.swapaxes(held[t, :, at, :], 0, 1) for t in range(nt)]
-            sums = list(sums)
-            for shift in range(diameter):
-                for b in range(mains):
+        lax.fori_loop(0, count // 4, four_rows, 0)
+
+    def turned(k, q, at):
+        return jnp.swapaxes(jnp.stack([held[k, turns * s + q, at, :] for s in range(8)]), 0, 1)
+
+    def make(b):
+        used = [
+            t
+            for t in range(nt)
+            if STRIDE * (t + 1) - reach > LANES * b - reach
+            and STRIDE * t - reach < LANES * (b + 1) + reach
+        ]
+        traces(m_ref, rows + 2 * reach, used)
+
+        def one_vector(q, carry):
+            def some_times(n, total):
+                at = pl.ds(pl.multiple_of(8 * n, 8), 8)
+                tiles = [-turned(k, q, at) for k in range(len(used))]
+                for shift in range(diameter):
                     low = LANES * b + shift - reach
                     value = None
-                    for t in range(nt):
+                    for t, tile in zip(used, tiles):
                         begin, end = STRIDE * t - reach, STRIDE * (t + 1) - reach
                         if end <= low or begin >= low + LANES:
                             continue
                         turn = (STRIDE * t - HALO - low) % LANES
-                        moved = pltpu.roll(tiles[t], turn, 2) if turn else tiles[t]
+                        moved = pltpu.roll(tile, turn, 2) if turn else tile
                         value = (
                             moved
                             if value is None
                             else jnp.where(lane < begin - low, value, moved)
                         )
-                    shifted[shift, at, b, here, :] = value
-                    sums[b] = sums[b] + jnp.sum(value * value, axis=0)
-            return tuple(sums)
-
-        zero = jnp.zeros((8, LANES), jnp.float32)
-        sums = lax.fori_loop(0, samples // 8, some_times, (zero,) * mains)
-        for b in range(mains):
-            power[b, here, :] = sums[b]
+                    shifted[q, shift, at] = value
+                    total = total + jnp.sum(value * value, axis=0)
+                return total
+
+            power[q] = lax.fori_loop(
+                0, samples // 8, some_times, jnp.zeros((8, LANES), jnp.float32)
+            )
+            return carry
+
+        lax.fori_loop(0, turns + 2 * reach, one_vector, 0)
+        traces(d_ref, rows, [b])
+
+    for b in range(width // LANES):
+        pl.when(pl.program_id(0) == b)(functools.partial(make, b))
+
+    def turn_data(q, carry):
+        for n in range(samples // 8):
+            data[q, 8 * n : 8 * n + 8] = turned(0, q, slice(8 * n, 8 * n + 8))
         return carry
 
-    lax.fori_loop(jnp.where(i == 0, 0, i + 1), i + 2, make_block, 0)
-
-    traces(d_ref, 8 * i, mains)
-
-    def turn_data(n, carry):
-        at = pl.ds(pl.multiple_of(8 * n, 8), 8)
-        for b in range(mains):
-            data[at, b] = jnp.swapaxes(held[b, :, at, :], 0, 1)
-        return carry
-
-    lax.fori_loop(0, samples // 8, turn_data, 0)
+    lax.fori_loop(0, turns, turn_data, 0)
 
     taps = [(a, c) for a in range(diameter) for c in range(diameter)]
-
-    def one_tile(b, carry):
+    together = 4
+
+    def one_vector(q, carry):
         def tap(t, a, c):
-            return shifted[c, t, b, pl.ds(8 * i + a, 8), :]
+            return shifted[q + a, c, t]
 
         energy = energy_floor
         for a in range(diameter):
-            energy = energy + power[b, pl.ds(8 * i + a, 8), :]
+            energy = energy + power[q + a]
         gain = step_size / energy
 
         def match(read):
             def some(n, sums):
                 sums = list(sums)
-                for u in range(2):
-                    t = 2 * n + u
+                for u in range(together):
+                    t = together * n + u
                     value = read(t)
                     sums = [sums[k] + value * tap(t, a, c) for k, (a, c) in enumerate(taps)]
                 return tuple(sums)
 
             zero = jnp.zeros((8, LANES), jnp.float32)
-            sums = lax.fori_loop(0, samples // 2, some, (zero,) * len(taps))
+            sums = lax.fori_loop(0, samples // together, some, (zero,) * len(taps))
             return [found * gain for found in sums]
 
         def remove(weights, write):
             def some(n, carry):
-                for u in range(2):
-                    t = 2 * n + u
+                for u in range(together):
+                    t = together * n + u
                     parts = [None] * diameter
                     for weight, (a, c) in zip(weights, taps):
                         term = weight * tap(t, a, c)
                         parts[c] = term if parts[c] is None else parts[c] + term
                     filtered = functools.reduce(jnp.add, parts)
-                    write(t, data[t, b] - filtered)
+                    write(t, data[q, t] - filtered)
                 return carry
 
-            lax.fori_loop(0, samples // 2, some, 0)
+            lax.fori_loop(0, samples // together, some, 0)
 
         def keep(t, value):
             residual[t] = value
 
-        at = pl.ds(pl.multiple_of(b * LANES, LANES), LANES)
+        at = pl.ds(q, 8, stride=turns)
 
         def put(t, value):
-            p_ref[t, :, at] = value
-            q_ref[t, :, at] = tap(t, reach, reach)
-
-        weights = match(lambda t: data[t, b])
+            p_ref[t, at, :] = value
+            q_ref[t, at, :] = tap(t, reach, reach)
+
+        weights = match(lambda t: data[q, t])
         for repeat in range(1, PASSES):
             remove(weights, keep)
             weights = [w + more for w, more in zip(weights, match(lambda t: residual[t]))]
         remove(weights, put)
         return carry
 
-    lax.fori_loop(0, mains, one_tile, 0)
+    lax.fori_loop(0, turns, one_vector, 0)
 
 
 def local(mesh_shape, data_spectrum, velocity_level):
@@ -595,20 +610,21 @@
         name="predict",
     )(data_spectrum, strips, levels, table)
 
-    block = pl.BlockSpec((samples, 8, width), lambda i: (0, i, 0))
+    block = pl.BlockSpec((samples, rows, LANES), lambda b: (0, 0, b))
     out = jax.ShapeDtypeStruct((samples, rows, width), jnp.float32)
+    turns = rows // 8
     return pl.pallas_call(
         functools.partial(subtract_kernel, rows, width),
-        grid=(rows // 8,),
+        grid=(mains,),
         out_shape=(out, out),
         in_specs=[vmem, vmem, vmem],
         out_specs=(block, block),
         scratch_shapes=[
-            pltpu.VMEM((2 * reach + 1, samples, mains, rows + 8, LANES), jnp.float32),
-            pltpu.VMEM((mains, rows + 8, LANES), jnp.float32),
-            pltpu.VMEM((samples, mains, 8, LANES), jnp.float32),
+            pltpu.VMEM((turns + 2 * reach, 2 * reach + 1, samples, 8, LANES), jnp.float32),
+            pltpu.VMEM((turns + 2 * reach, 8, LANES), jnp.float32),
+            pltpu.VMEM((turns, samples, 8, LANES), jnp.float32),
             pltpu.VMEM((samples, 8, LANES), jnp.float32),
-            pltpu.VMEM((nt, 8, samples, LANES), jnp.float32),
+            pltpu.VMEM((nt, rows + 2 * reach, samples, LANES), jnp.float32),
         ],
         compiler_params=pltpu.CompilerParams(vmem_limit_bytes=56 * 2**20),
         name="subtract",

time: 311 us -> 291 us (0.936)
  Pallas kernels: 302 us -> 282 us
    pallas_call x1, Pallas kernels: 181 us -> 162 us  [local(): pl.pallas_call(functools.partial(predict_kernel, tiles, nz, per_chunk, ch...]
where the time goes in v3:
time: 291 us
  Pallas kernels  282 us (97%)
  local copies, waits for them, and re-layouts  6.93 us (2%)
    pallas_call x1, Pallas kernels, local(): pl.pallas_call(functools.partial(predict_kernel, tiles, nz, per_chunk, ch...  162 us
    pallas_call x1, Pallas kernels, local(): pl.pallas_call(functools.partial(subtract_kernel, rows, width), grid=(mai...  120 us

profile of v3, /device:TPU:11, one launch (start us, length us, event | category | flops | bytes accessed | tf_op | source)
XLA Modules:
  0.0 291.0 jit_solution(16829558984960587449)
XLA Ops:
  0.6 1.7 pad.8.level_ref
  2.3 2.4 fusion
  4.7 0.2 concatenate.13
  5.0 0.2 copy.13
  5.2 0.9 copy.10
  6.1 0.3 pad_maximum_fusion.1
  6.4 0.2 copy.11
  6.6 0.2 copy.12
  6.8 1.1 pad_maximum_fusion
  7.9 1.1 copy.14.strip_ref
  9.0 162.1 %predict.1 = (f32[72,3,2,4,8,128]{5,4,3,2,1,0:T(8,128)}, f32[64,2,2,4,8,128]{5,4,3,2,1,0:T(8,128)}) custom-call(f32[2,8,64,1024]{3,2,1,0:T(8,128)} %x_ref.1, f32[4,4,64,128]{3,2,1,0:T(8,128)} %copy.14.strip_ref, s32[64,1280]{1,0:T(8,128)} %pad.8.level_ref, f32[4,4,8,128]{3,2,1,0:T(8,128)} %constant.9.clone.table_ref), custom_call_target="tpu_custom_call" | custom-call | tf_op jit(solution)/shard_map/predict/pallas_call | solution.py:587
  171.1 119.8 %subtract.1 = (f32[64,64,256]{2,1,0:T(8,128)}, f32[64,64,256]{2,1,0:T(8,128)}) custom-call(f32[72,3,2,4,8,128]{5,4,3,2,1,0:T(8,128)} %get-tuple-element.4.m_ref, f32[64,2,2,4,8,128]{5,4,3,2,1,0:T(8,128)} %get-tuple-element.5.d_ref, bf16[64,256]{1,0:T(8,128)(2,1)} %constant.10.clone.basis_ref), custom_call_target="tpu_custom_call" | custom-call | tf_op jit(solution)/shard_map/subtract/pallas_call | solution.py:616
  (1 shorter events, 0.0 us)

commit v4 on v3

--- a/solution.py
+++ b/solution.py
@@ -25,6 +25,7 @@
 HALO = 16
 LANES = 128
 ROWS = 12
+PAIR = 2
 STRIDE = 100
 OUTSIDE = 127
 MESH = pl.DeviceIdType.MESH
@@ -81,7 +82,7 @@
     basis = basis.astype(np.float32)
     high = basis.astype(ml_dtypes.bfloat16)
     low = (basis - high.astype(np.float32)).astype(ml_dtypes.bfloat16)
-    return np.concatenate([high, high, low, low], axis=1)
+    return np.concatenate([high, high, low], axis=1)
 
 
 def predict_kernel(
@@ -281,9 +282,7 @@
             for copy in row_copies(j, False):
                 copy.start()
 
-    arrive(0)
-
-    def one_chunk(j, carry):
+    def make_coefs(j):
         def make_coef(b, carry):
             values = [table_ref[j, c] for c in range(4)]
             for r in range(8):
@@ -296,6 +295,12 @@
             return carry
 
         lax.fori_loop(0, full // 8, make_coef, 0)
+
+    make_coefs(0)
+    arrive(0)
+
+    def one_chunk(j, carry):
+        pl.when(j > 0)(functools.partial(make_coefs, j))
 
         @pl.when(has_up)
         def _():
@@ -408,7 +413,7 @@
 def to_trace(basis, spectrum):
     high = spectrum.astype(jnp.bfloat16)
     low = (spectrum - high.astype(jnp.float32)).astype(jnp.bfloat16)
-    both = jnp.concatenate([high, low, high, low], axis=0)
+    both = jnp.concatenate([high, low, high], axis=0)
     return jnp.dot(basis, both, preferred_element_type=jnp.float32)
 
 
@@ -491,61 +496,72 @@
     lax.fori_loop(0, turns, turn_data, 0)
 
     taps = [(a, c) for a in range(diameter) for c in range(diameter)]
-    together = 4
-
-    def one_vector(q, carry):
-        def tap(t, a, c):
-            return shifted[q + a, c, t]
-
-        energy = energy_floor
-        for a in range(diameter):
-            energy = energy + power[q + a]
-        gain = step_size / energy
+    zero = jnp.zeros((8, LANES), jnp.float32)
+
+    def vector_pair(n, carry):
+        first = PAIR * n
+        pair = range(PAIR)
+
+        def column(t, c):
+            return [shifted[first + a, c, t] for a in range(diameter + PAIR - 1)]
+
+        gains = []
+        for v in pair:
+            energy = energy_floor
+            for a in range(diameter):
+                energy = energy + power[first + v + a]
+            gains.append(step_size / energy)
 
         def match(read):
-            def some(n, sums):
-                sums = list(sums)
-                for u in range(together):
-                    t = together * n + u
-                    value = read(t)
-                    sums = [sums[k] + value * tap(t, a, c) for k, (a, c) in enumerate(taps)]
-                return tuple(sums)
-
-            zero = jnp.zeros((8, LANES), jnp.float32)
-            sums = lax.fori_loop(0, samples // together, some, (zero,) * len(taps))
-            return [found * gain for found in sums]
+            def some(t, sums):
+                values = [read(v, t) for v in pair]
+                sums = [list(part) for part in sums]
+                for c in range(diameter):
+                    cells = column(t, c)
+                    for a in range(diameter):
+                        for v in pair:
+                            k = a * diameter + c
+                            sums[v][k] = sums[v][k] + values[v] * cells[v + a]
+                return tuple(tuple(part) for part in sums)
+
+            sums = lax.fori_loop(0, samples, some, ((zero,) * len(taps),) * PAIR, unroll=2)
+            return [[found * gains[v] for found in sums[v]] for v in pair]
 
         def remove(weights, write):
-            def some(n, carry):
-                for u in range(together):
-                    t = together * n + u
-                    parts = [None] * diameter
-                    for weight, (a, c) in zip(weights, taps):
-                        term = weight * tap(t, a, c)
-                        parts[c] = term if parts[c] is None else parts[c] + term
-                    filtered = functools.reduce(jnp.add, parts)
-                    write(t, data[q, t] - filtered)
+            def some(t, carry):
+                filtered = [None] * PAIR
+                for c in range(diameter):
+                    cells = column(t, c)
+                    for v in pair:
+                        part = weights[v][c] * cells[v]
+                        for a in range(1, diameter):
+                            part = part + weights[v][a * diameter + c] * cells[v + a]
+                        filtered[v] = part if c == 0 else filtered[v] + part
+                for v in pair:
+                    write(v, t, data[first + v, t] - filtered[v])
                 return carry
 
-            lax.fori_loop(0, samples // together, some, 0)
-
-        def keep(t, value):
-            residual[t] = value
-
-        at = pl.ds(q, 8, stride=turns)
-
-        def put(t, value):
+            lax.fori_loop(0, samples, some, 0, unroll=2)
+
+        def keep(v, t, value):
+            residual[v, t] = value
+
+        def put(v, t, value):
+            at = pl.ds(first + v, 8, stride=turns)
             p_ref[t, at, :] = value
-            q_ref[t, at, :] = tap(t, reach, reach)
-
-        weights = match(lambda t: data[q, t])
+            q_ref[t, at, :] = shifted[first + v + reach, reach, t]
+
+        weights = match(lambda v, t: data[first + v, t])
         for repeat in range(1, PASSES):
             remove(weights, keep)
-            weights = [w + more for w, more in zip(weights, match(lambda t: residual[t]))]
+            change = match(lambda v, t: residual[v, t])
+            weights = [
+                [w + more for w, more in zip(weights[v], change[v])] for v in pair
+            ]
         remove(weights, put)
         return carry
 
-    lax.fori_loop(0, turns, one_vector, 0)
+    lax.fori_loop(0, turns // PAIR, vector_pair, 0)
 
 
 def local(mesh_shape, data_spectrum, velocity_level):
@@ -623,7 +639,7 @@
             pltpu.VMEM((turns + 2 * reach, 2 * reach + 1, samples, 8, LANES), jnp.float32),
             pltpu.VMEM((turns + 2 * reach, 8, LANES), jnp.float32),
             pltpu.VMEM((turns, samples, 8, LANES), jnp.float32),
-            pltpu.VMEM((samples, 8, LANES), jnp.float32),
+            pltpu.VMEM((PAIR, samples, 8, LANES), jnp.float32),
             pltpu.VMEM((nt, rows + 2 * reach, samples, LANES), jnp.float32),
         ],
         compiler_params=pltpu.CompilerParams(vmem_limit_bytes=56 * 2**20),

time: 291 us -> 304 us (1.045)
  Pallas kernels: 282 us -> 295 us
    pallas_call x1, Pallas kernels: 120 us -> 133 us  [local(): pl.pallas_call(functools.partial(subtract_kernel, rows, width), grid=(mai...]
where the time goes in v4:
time: 304 us
  Pallas kernels  295 us (97%)
  local copies, waits for them, and re-layouts  6.93 us (2%)
    pallas_call x1, Pallas kernels, local(): pl.pallas_call(functools.partial(predict_kernel, tiles, nz, per_chunk, ch...  162 us
    pallas_call x1, Pallas kernels, local(): pl.pallas_call(functools.partial(subtract_kernel, rows, width), grid=(mai...  133 us

profile of v4, /device:TPU:11, one launch (start us, length us, event | category | flops | bytes accessed | tf_op | source)
XLA Modules:
  0.0 303.7 jit_solution(10656683094894746875)
XLA Ops:
  0.6 1.7 pad.8.level_ref
  2.3 2.4 fusion
  4.7 0.2 concatenate.13
  5.0 0.2 copy.13
  5.2 0.9 copy.10
  6.1 0.3 pad_maximum_fusion.1
  6.4 0.2 copy.11
  6.6 0.2 copy.12
  6.8 1.1 pad_maximum_fusion
  7.9 1.1 copy.14.strip_ref
  9.0 162.1 %predict.1 = (f32[72,3,2,4,8,128]{5,4,3,2,1,0:T(8,128)}, f32[64,2,2,4,8,128]{5,4,3,2,1,0:T(8,128)}) custom-call(f32[2,8,64,1024]{3,2,1,0:T(8,128)} %x_ref.1, f32[4,4,64,128]{3,2,1,0:T(8,128)} %copy.14.strip_ref, s32[64,1280]{1,0:T(8,128)} %pad.8.level_ref, f32[4,4,8,128]{3,2,1,0:T(8,128)} %constant.9.clone.table_ref), custom_call_target="tpu_custom_call" | custom-call | tf_op jit(solution)/shard_map/predict/pallas_call | solution.py:603
  171.1 132.5 %subtract.1 = (f32[64,64,256]{2,1,0:T(8,128)}, f32[64,64,256]{2,1,0:T(8,128)}) custom-call(f32[72,3,2,4,8,128]{5,4,3,2,1,0:T(8,128)} %get-tuple-element.4.m_ref, f32[64,2,2,4,8,128]{5,4,3,2,1,0:T(8,128)} %get-tuple-element.5.d_ref, bf16[64,192]{1,0:T(8,128)(2,1)} %constant.10.clone.basis_ref), custom_call_target="tpu_custom_call" | custom-call | tf_op jit(solution)/shard_map/subtract/pallas_call | solution.py:632
  (1 shorter events, 0.0 us)

commit v5 on v3

--- a/solution.py
+++ b/solution.py
@@ -25,6 +25,7 @@
 HALO = 16
 LANES = 128
 ROWS = 12
+TOGETHER = 4
 STRIDE = 100
 OUTSIDE = 127
 MESH = pl.DeviceIdType.MESH
@@ -81,7 +82,7 @@
     basis = basis.astype(np.float32)
     high = basis.astype(ml_dtypes.bfloat16)
     low = (basis - high.astype(np.float32)).astype(ml_dtypes.bfloat16)
-    return np.concatenate([high, high, low, low], axis=1)
+    return np.concatenate([high, high, low], axis=1)
 
 
 def predict_kernel(
@@ -408,144 +409,123 @@
 def to_trace(basis, spectrum):
     high = spectrum.astype(jnp.bfloat16)
     low = (spectrum - high.astype(jnp.float32)).astype(jnp.bfloat16)
-    both = jnp.concatenate([high, low, high, low], axis=0)
+    both = jnp.concatenate([high, low, high], axis=0)
     return jnp.dot(basis, both, preferred_element_type=jnp.float32)
 
 
 def subtract_kernel(
-    rows, width, m_ref, d_ref, basis_ref, p_ref, q_ref, shifted, power, data, residual, held
+    rows, width, m_ref, d_ref, basis_ref, p_ref, q_ref, shifted, power, data, result
 ):
+    i = pl.program_id(0)
+    mains = width // LANES
     nt = m_ref.shape[1]
     reach = filter_reach
     diameter = 2 * reach + 1
     samples = basis_ref.shape[0]
-    turns = rows // 8
     basis = basis_ref[...]
-    lane = lax.broadcasted_iota(jnp.int32, (8, 8, LANES), 2)
-
-    def traces(ref, count, tiles):
-        def four_rows(n, carry):
-            spectrum = jnp.concatenate(
-                [ref[4 * n + r, t].reshape(samples, LANES) for r in range(4) for t in tiles],
-                axis=1,
-            )
-            found = to_trace(basis, spectrum)
-            for r in range(4):
-                for k in range(len(tiles)):
-                    at = (r * len(tiles) + k) * LANES
-                    held[k, 4 * n + r] = found[:, at : at + LANES]
-            return carry
-
-        lax.fori_loop(0, count // 4, four_rows, 0)
-
-    def turned(k, q, at):
-        return jnp.swapaxes(jnp.stack([held[k, turns * s + q, at, :] for s in range(8)]), 0, 1)
-
-    def make(b):
-        used = [
-            t
-            for t in range(nt)
-            if STRIDE * (t + 1) - reach > LANES * b - reach
-            and STRIDE * t - reach < LANES * (b + 1) + reach
+    lane = lax.broadcasted_iota(jnp.int32, (samples, LANES), 1)
+
+    def traces(ref, first, count):
+        spectrum = jnp.concatenate(
+            [
+                ref[first + r, t].reshape(samples, LANES)
+                for r in range(TOGETHER)
+                for t in range(count)
+            ],
+            axis=1,
+        )
+        found = to_trace(basis, spectrum)
+        return [
+            [
+                found[:, (r * count + t) * LANES : (r * count + t + 1) * LANES]
+                for t in range(count)
+            ]
+            for r in range(TOGETHER)
         ]
-        traces(m_ref, rows + 2 * reach, used)
-
-        def one_vector(q, carry):
-            def some_times(n, total):
-                at = pl.ds(pl.multiple_of(8 * n, 8), 8)
-                tiles = [-turned(k, q, at) for k in range(len(used))]
+
+    def make_rows(n, carry):
+        for r, tiles in enumerate(traces(m_ref, TOGETHER * n, nt)):
+            row = TOGETHER * n + r
+            for b in range(mains):
+                total = None
                 for shift in range(diameter):
                     low = LANES * b + shift - reach
                     value = None
-                    for t, tile in zip(used, tiles):
+                    for t in range(nt):
                         begin, end = STRIDE * t - reach, STRIDE * (t + 1) - reach
                         if end <= low or begin >= low + LANES:
                             continue
                         turn = (STRIDE * t - HALO - low) % LANES
-                        moved = pltpu.roll(tile, turn, 2) if turn else tile
+                        moved = pltpu.roll(tiles[t], turn, 1) if turn else tiles[t]
                         value = (
                             moved
                             if value is None
                             else jnp.where(lane < begin - low, value, moved)
                         )
-                    shifted[q, shift, at] = value
-                    total = total + jnp.sum(value * value, axis=0)
-                return total
-
-            power[q] = lax.fori_loop(
-                0, samples // 8, some_times, jnp.zeros((8, LANES), jnp.float32)
+                    value = -value
+                    shifted[shift, b, row] = value
+                    part = jnp.sum((value * value).reshape(samples // 8, 8, LANES), axis=0)
+                    total = part if total is None else total + part
+                power[b, row] = total
+        return carry
+
+    lax.fori_loop(
+        jnp.where(i == 0, 0, (8 * i + 2 * reach) // TOGETHER),
+        (8 * i + 8 + 2 * reach) // TOGETHER,
+        make_rows,
+        0,
+    )
+
+    def make_data(n, carry):
+        for r, tiles in enumerate(traces(d_ref, 8 * i + TOGETHER * n, mains)):
+            for b in range(mains):
+                data[b, TOGETHER * n + r] = tiles[b]
+        return carry
+
+    lax.fori_loop(0, 8 // TOGETHER, make_data, 0)
+
+    taps = [(a, c) for a in range(diameter) for c in range(diameter)]
+
+    def total(values):
+        return jnp.sum(values, axis=0, keepdims=True)
+
+    def one_row(n, carry):
+        r, b = n // mains, lax.rem(n, mains)
+
+        def tap(a, c):
+            return shifted[c, b, 8 * i + r + a]
+
+        recorded = data[b, r]
+        energy = power[b, 8 * i + r]
+        for a in range(1, diameter):
+            energy = energy + power[b, 8 * i + r + a]
+        gain = step_size / (energy_floor + total(energy))
+
+        def remove(weights):
+            residual = recorded
+            for weight, (a, c) in zip(weights, taps):
+                residual = residual - weight * tap(a, c)
+            return residual
+
+        weights = [total(recorded * tap(a, c)) * gain for a, c in taps]
+        for repeat in range(1, PASSES):
+            residual = remove(weights)
+            weights = [
+                w + total(residual * tap(a, c)) * gain for w, (a, c) in zip(weights, taps)
+            ]
+        result[b, r] = remove(weights)
+        return carry
+
+    lax.fori_loop(0, 8 * mains, one_row, 0)
+
+    for b in range(mains):
+        at = slice(b * LANES, (b + 1) * LANES)
+        for k in range(samples // 8):
+            part = slice(8 * k, 8 * k + 8)
+            p_ref[part, :, at] = jnp.swapaxes(result[b, :, part, :], 0, 1)
+            q_ref[part, :, at] = jnp.swapaxes(
+                shifted[reach, b, pl.ds(8 * i + reach, 8), part, :], 0, 1
             )
-            return carry
-
-        lax.fori_loop(0, turns + 2 * reach, one_vector, 0)
-        traces(d_ref, rows, [b])
-
-    for b in range(width // LANES):
-        pl.when(pl.program_id(0) == b)(functools.partial(make, b))
-
-    def turn_data(q, carry):
-        for n in range(samples // 8):
-            data[q, 8 * n : 8 * n + 8] = turned(0, q, slice(8 * n, 8 * n + 8))
-        return carry
-
-    lax.fori_loop(0, turns, turn_data, 0)
-
-    taps = [(a, c) for a in range(diameter) for c in range(diameter)]
-    together = 4
-
-    def one_vector(q, carry):
-        def tap(t, a, c):
-            return shifted[q + a, c, t]
-
-        energy = energy_floor
-        for a in range(diameter):
-            energy = energy + power[q + a]
-        gain = step_size / energy
-
-        def match(read):
-            def some(n, sums):
-                sums = list(sums)
-                for u in range(together):
-                    t = together * n + u
-                    value = read(t)
-                    sums = [sums[k] + value * tap(t, a, c) for k, (a, c) in enumerate(taps)]
-                return tuple(sums)
-
-            zero = jnp.zeros((8, LANES), jnp.float32)
-            sums = lax.fori_loop(0, samples // together, some, (zero,) * len(taps))
-            return [found * gain for found in sums]
-
-        def remove(weights, write):
-            def some(n, carry):
-                for u in range(together):
-                    t = together * n + u
-                    parts = [None] * diameter
-                    for weight, (a, c) in zip(weights, taps):
-                        term = weight * tap(t, a, c)
-                        parts[c] = term if parts[c] is None else parts[c] + term
-                    filtered = functools.reduce(jnp.add, parts)
-                    write(t, data[q, t] - filtered)
-                return carry
-
-            lax.fori_loop(0, samples // together, some, 0)
-
-        def keep(t, value):
-            residual[t] = value
-
-        at = pl.ds(q, 8, stride=turns)
-
-        def put(t, value):
-            p_ref[t, at, :] = value
-            q_ref[t, at, :] = tap(t, reach, reach)
-
-        weights = match(lambda t: data[q, t])
-        for repeat in range(1, PASSES):
-            remove(weights, keep)
-            weights = [w + more for w, more in zip(weights, match(lambda t: residual[t]))]
-        remove(weights, put)
-        return carry
-
-    lax.fori_loop(0, turns, one_vector, 0)
 
 
 def local(mesh_shape, data_spectrum, velocity_level):
@@ -610,21 +590,19 @@
         name="predict",
     )(data_spectrum, strips, levels, table)
 
-    block = pl.BlockSpec((samples, rows, LANES), lambda b: (0, 0, b))
+    block = pl.BlockSpec((samples, 8, width), lambda i: (0, i, 0))
     out = jax.ShapeDtypeStruct((samples, rows, width), jnp.float32)
-    turns = rows // 8
     return pl.pallas_call(
         functools.partial(subtract_kernel, rows, width),
-        grid=(mains,),
+        grid=(rows // 8,),
         out_shape=(out, out),
         in_specs=[vmem, vmem, vmem],
         out_specs=(block, block),
         scratch_shapes=[
-            pltpu.VMEM((turns + 2 * reach, 2 * reach + 1, samples, 8, LANES), jnp.float32),
-            pltpu.VMEM((turns + 2 * reach, 8, LANES), jnp.float32),
-            pltpu.VMEM((turns, samples, 8, LANES), jnp.float32),
-            pltpu.VMEM((samples, 8, LANES), jnp.float32),
-            pltpu.VMEM((nt, rows + 2 * reach, samples, LANES), jnp.float32),
+            pltpu.VMEM((2 * reach + 1, mains, rows + 2 * reach, samples, LANES), jnp.float32),
+            pltpu.VMEM((mains, rows + 2 * reach, 8, LANES), jnp.float32),
+            pltpu.VMEM((mains, 8, samples, LANES), jnp.float32),
+            pltpu.VMEM((mains, 8, samples, LANES), jnp.float32),
         ],
         compiler_params=pltpu.CompilerParams(vmem_limit_bytes=56 * 2**20),
         name="subtract",

time: 291 us -> 247 us (0.85)
  Pallas kernels: 282 us -> 237 us
    pallas_call x1, Pallas kernels: 120 us -> 75.2 us  [local(): pl.pallas_call(functools.partial(subtract_kernel, rows, width), grid=(row...]
where the time goes in v5:
time: 247 us; the launch traced here: 246 us
  Pallas kernels  237 us (96%)
  local copies, waits for them, and re-layouts  6.93 us (3%)
    pallas_call x1, Pallas kernels, local(): pl.pallas_call(functools.partial(predict_kernel, tiles, nz, per_chunk, ch...  162 us
    pallas_call x1, Pallas kernels, local(): pl.pallas_call(functools.partial(subtract_kernel, rows, width), grid=(row...  75.2 us

profile of v5, /device:TPU:11, one launch (start us, length us, event | category | flops | bytes accessed | tf_op | source)
XLA Modules:
  0.0 246.3 jit_solution(4752569636136843959)
XLA Ops:
  0.6 1.7 pad.8.level_ref
  2.3 2.4 fusion
  4.7 0.2 concatenate.13
  5.0 0.2 copy.13
  5.2 0.9 copy.10
  6.1 0.3 pad_maximum_fusion.1
  6.4 0.2 copy.11
  6.6 0.2 copy.12
  6.8 1.1 pad_maximum_fusion
  7.9 1.1 copy.14.strip_ref
  9.0 162.1 %predict.1 = (f32[72,3,2,4,8,128]{5,4,3,2,1,0:T(8,128)}, f32[64,2,2,4,8,128]{5,4,3,2,1,0:T(8,128)}) custom-call(f32[2,8,64,1024]{3,2,1,0:T(8,128)} %x_ref.1, f32[4,4,64,128]{3,2,1,0:T(8,128)} %copy.14.strip_ref, s32[64,1280]{1,0:T(8,128)} %pad.8.level_ref, f32[4,4,8,128]{3,2,1,0:T(8,128)} %constant.9.clone.table_ref), custom_call_target="tpu_custom_call" | custom-call | tf_op jit(solution)/shard_map/predict/pallas_call | solution.py:567
  171.1 75.2 %subtract.1 = (f32[64,64,256]{2,1,0:T(8,128)}, f32[64,64,256]{2,1,0:T(8,128)}) custom-call(f32[72,3,2,4,8,128]{5,4,3,2,1,0:T(8,128)} %get-tuple-element.4.m_ref, f32[64,2,2,4,8,128]{5,4,3,2,1,0:T(8,128)} %get-tuple-element.5.d_ref, bf16[64,192]{1,0:T(8,128)(2,1)} %constant.10.clone.basis_ref), custom_call_target="tpu_custom_call" | custom-call | tf_op jit(solution)/shard_map/subtract/pallas_call | solution.py:595
  (1 shorter events, 0.0 us)

commit v6 on v5

--- a/solution.py
+++ b/solution.py
@@ -24,7 +24,7 @@
 
 HALO = 16
 LANES = 128
-ROWS = 12
+ROWS = 16
 TOGETHER = 4
 STRIDE = 100
 OUTSIDE = 127
@@ -489,9 +489,12 @@
     def total(values):
         return jnp.sum(values, axis=0, keepdims=True)
 
-    def one_row(n, carry):
-        r, b = n // mains, lax.rem(n, mains)
-
+    def one_row(r, carry):
+        for b in range(mains):
+            one_tile(r, b)
+        return carry
+
+    def one_tile(r, b):
         def tap(a, c):
             return shifted[c, b, 8 * i + r + a]
 
@@ -514,9 +517,8 @@
                 w + total(residual * tap(a, c)) * gain for w, (a, c) in zip(weights, taps)
             ]
         result[b, r] = remove(weights)
-        return carry
-
-    lax.fori_loop(0, 8 * mains, one_row, 0)
+
+    lax.fori_loop(0, 8, one_row, 0)
 
     for b in range(mains):
         at = slice(b * LANES, (b + 1) * LANES)

time: 247 us -> 243 us (0.984)
  Pallas kernels: 237 us -> 234 us
    pallas_call x1, Pallas kernels: 162 us -> 158 us  [local(): pl.pallas_call(functools.partial(predict_kernel, tiles, nz, per_chunk, ch...]
where the time goes in v6:
time: 243 us
  Pallas kernels  234 us (96%)
  local copies, waits for them, and re-layouts  6.93 us (3%)
    pallas_call x1, Pallas kernels, local(): pl.pallas_call(functools.partial(predict_kernel, tiles, nz, per_chunk, ch...  158 us
    pallas_call x1, Pallas kernels, local(): pl.pallas_call(functools.partial(subtract_kernel, rows, width), grid=(row...  75.7 us

profile of v6, /device:TPU:11, one launch (start us, length us, event | category | flops | bytes accessed | tf_op | source)
XLA Modules:
  0.0 242.9 jit_solution(9121194410171401145)
XLA Ops:
  0.6 1.7 pad.8.level_ref
  2.3 2.4 fusion
  4.7 0.2 concatenate.13
  5.0 0.2 copy.13
  5.2 0.9 copy.10
  6.1 0.3 pad_maximum_fusion.1
  6.4 0.2 copy.11
  6.6 0.2 copy.12
  6.8 1.1 pad_maximum_fusion
  7.9 1.1 copy.14.strip_ref
  9.0 158.2 %predict.1 = (f32[72,3,2,4,8,128]{5,4,3,2,1,0:T(8,128)}, f32[64,2,2,4,8,128]{5,4,3,2,1,0:T(8,128)}) custom-call(f32[2,8,64,1024]{3,2,1,0:T(8,128)} %x_ref.1, f32[4,4,64,128]{3,2,1,0:T(8,128)} %copy.14.strip_ref, s32[64,1280]{1,0:T(8,128)} %pad.8.level_ref, f32[4,4,8,128]{3,2,1,0:T(8,128)} %constant.9.clone.table_ref), custom_call_target="tpu_custom_call" | custom-call | tf_op jit(solution)/shard_map/predict/pallas_call | solution.py:569
  167.2 75.7 %subtract.1 = (f32[64,64,256]{2,1,0:T(8,128)}, f32[64,64,256]{2,1,0:T(8,128)}) custom-call(f32[72,3,2,4,8,128]{5,4,3,2,1,0:T(8,128)} %get-tuple-element.4.m_ref, f32[64,2,2,4,8,128]{5,4,3,2,1,0:T(8,128)} %get-tuple-element.5.d_ref, bf16[64,192]{1,0:T(8,128)(2,1)} %constant.10.clone.basis_ref), custom_call_target="tpu_custom_call" | custom-call | tf_op jit(solution)/shard_map/subtract/pallas_call | solution.py:597
  (1 shorter events, 0.0 us)
